TPU v7x, 128 devices: a whole 4x4x4 slice. The times are simulated.
128 devices in a mesh: replica: 16 (over y, z_hi, core), fsdp: 8 (over x, z_lo).
Axes of the slice: x: 4, y: 4, z: 4 (z_hi: 2, z_lo: 2; z = z_hi * 2 + z_lo), core: 2. Of those that a mesh axis runs over, the one named last changes fastest.
Arguments:
- tokens: bfloat16 [16, 3072, 8192], P('replica', 'fsdp'), may hold values from -6 to 6
- queries: bfloat16 [16, 3072, 4096], P('replica', 'fsdp'), may hold values from -250 to 250
- kv_weight: bfloat16 [16, 8192, 1024], P('replica', 'fsdp'), may hold values from -0.06629126 to 0.06629126
- doc_lengths: int32 [16, 8, 6], P('replica', 'fsdp'), may hold values from 1 to 192, 384 in all within a row
- local_params: bfloat16 [16, 1536, 8192], P('replica', 'fsdp'), may hold values from -6 to 6
- base_copy: bfloat16 [1536, 8192], P('fsdp'), may hold values from -6 to 6
- master: float32 [1536, 8192], P('fsdp', 'replica'), may hold values from -6 to 6
- momentum: float32 [1536, 8192], P('fsdp', 'replica'), may hold values from -2 to 2
Outputs:
- attended: bfloat16 [16, 3072, 4096], P('replica', 'fsdp')
- new_master: float32 [1536, 8192], P('fsdp', 'replica')
- new_momentum: float32 [1536, 8192], P('fsdp', 'replica')
- fresh_params: bfloat16 [1536, 8192], P('fsdp')
Inputs may be any that keep to these rules, and one draw needn't show every extreme that they name: `doc_lengths`: each device's 6 lengths sum to 384, and the longest is exactly 192.
All inputs are finite; a program needn't handle non-finite values.
Results may differ from a plain program's by a relative error of at most 0.012.
The roundings to bfloat16 on the way count: a program that leaves them out, or rounds other values in their place, can miss the bound.
Values may be sent and summed in bfloat16 or wider, within the bound.
A program may use at most 192 MiB of HBM per device.

v0:
```python
import jax
import jax.numpy as jnp
from jax import lax
from jax.sharding import Mesh
from jax.sharding import PartitionSpec as P

HEAD_SIZE = 128
BLK = 128
FSDP = ("fsdp_0", "fsdp_1")
MOMENTUM_COEF = 0.9
OUTER_RATE = 0.7
QUANT_RANGE = 448.0


def summed_rows(total, axes):
    for axis in axes:
        total = lax.psum_scatter(total, axis, scatter_dimension=0, tiled=True)
    return total


def doc_mask(lengths, tok_count):
    doc_ends = jnp.cumsum(lengths)
    places = jnp.arange(tok_count, dtype=jnp.int32)
    doc_index = jnp.sum((places[:, None] >= doc_ends[None, :-1]).astype(jnp.int32), axis=1)
    same_doc = doc_index[:, None] == doc_index[None, :]
    return jnp.logical_and(same_doc, places[None, :] <= places[:, None])


def attend(query_rows, packed, lengths):
    tok_count = query_rows.shape[0]
    head_count = query_rows.shape[1] // HEAD_SIZE
    groups = packed.shape[1] // (2 * HEAD_SIZE)
    key_heads = packed[:, : groups * HEAD_SIZE].reshape(tok_count, groups, HEAD_SIZE)
    value_heads = packed[:, groups * HEAD_SIZE :].reshape(tok_count, groups, HEAD_SIZE)
    grouped = query_rows.reshape(tok_count, groups, head_count // groups, HEAD_SIZE)
    scores = jnp.einsum(
        "tgjd,sgd->gjts", grouped, key_heads, preferred_element_type=jnp.float32
    ) * HEAD_SIZE ** (-0.5)
    allowed = doc_mask(lengths, tok_count)
    scores = jnp.where(allowed[None, None], scores, -1e30)
    highest = jnp.max(scores, axis=-1, keepdims=True)
    expo = jnp.exp(scores - highest)
    attn_weights = (expo / jnp.sum(expo, axis=-1, keepdims=True)).astype(jnp.bfloat16)
    mixed = jnp.einsum(
        "gjts,sgd->tgjd", attn_weights, value_heads, preferred_element_type=jnp.float32
    )
    return mixed.reshape(tok_count, head_count * HEAD_SIZE).astype(jnp.bfloat16)


def shards(tokens, queries, kv_weight, doc_lengths, local_params, base_copy, master, momentum):
    own_tokens = tokens[0]
    own_queries = queries[0]
    lengths = doc_lengths[0, 0]
    columns = lax.all_to_all(own_tokens, FSDP, split_axis=1, concat_axis=0, tiled=True)
    weight_shard = kv_weight[0]
    packed = summed_rows(jnp.dot(columns, weight_shard, preferred_element_type=jnp.float32), FSDP)
    attended = attend(own_queries, packed.astype(jnp.bfloat16), lengths)[None]
    replicas = lax.axis_size("replica")
    row_count = base_copy.shape[0]
    full_width = base_copy.shape[1]
    block_count = full_width // BLK
    pseudo_grad = base_copy.astype(jnp.float32) - local_params[0].astype(jnp.float32)
    blocked = pseudo_grad.reshape(row_count, block_count, BLK)
    scales = ((jnp.max(jnp.abs(blocked), axis=-1) + 1e-06) / QUANT_RANGE).astype(jnp.bfloat16)
    encoded = (blocked / scales.astype(jnp.float32)[..., None]).astype(jnp.bfloat16)
    decoded = (encoded.astype(jnp.float32) * scales.astype(jnp.float32)[..., None]).reshape(
        row_count, full_width
    )
    summed = lax.psum_scatter(
        decoded.astype(jnp.bfloat16), "replica", scatter_dimension=1, tiled=True
    ).astype(jnp.float32)
    averaged = summed * (1.0 / replicas)
    new_momentum = MOMENTUM_COEF * momentum + averaged
    new_master = master - OUTER_RATE * (averaged + MOMENTUM_COEF * new_momentum)
    fresh_params = lax.all_gather(new_master.astype(jnp.bfloat16), "replica", axis=1, tiled=True)
    return (attended, new_master, new_momentum, fresh_params)


def solution(mesh):
    finer = Mesh(mesh.devices.reshape(mesh.shape["replica"], 4, 2), ("replica", "fsdp_0", "fsdp_1"))
    placed = (
        P("replica", FSDP, None),
        P("replica", FSDP, None),
        P("replica", FSDP, None),
        P("replica", FSDP, None),
        P("replica", FSDP, None),
        P(FSDP, None),
        P(FSDP, "replica"),
        P(FSDP, "replica"),
    )
    return jax.shard_map(
        shards,
        mesh=finer,
        in_specs=placed,
        out_specs=(P("replica", FSDP, None), P(FSDP, "replica"), P(FSDP, "replica"), P(FSDP, None)),
        check_vma=False,
    )
```

profile of v0, /device:TPU:1, one launch (start us, length us, event | category | flops | bytes accessed | tf_op | source)
XLA Modules:
  0.0 413.3 jit_solution(16304995047222612006)
XLA Ops:
  7.2 0.0 copy-start
  7.2 8.8 %copy.29 = bf16[1,384,8192]{1,2,0:T(8,128)(2,1)} copy(bf16[1,384,8192]{2,1,0:T(8,128)(2,1)} %param.8) | data formatting | bytes 12582912 | tf_op args[0]
  16.0 6.2 %all-to-all-start = ((bf16[384,8,1024]{0,2,1:T(8,128)(2,1)}), bf16[384,8,1024]{0,2,1:T(8,128)(2,1)}, u32[]{:S(2)}, u32[]{:S(2)}) async-start(bf16[384,8,1024]{0,2,1:T(8,128)(2,1)} %bitcast.52), calls=%async_computation | async-start | bytes 12582912 | tf_op jit(solution)/shard_map/all_to_all | solution.py:54
  22.2 0.0 reduce-scatter.8.cloned.1.call-start
  22.2 4.0 abs_bitcast_fusion
  26.2 3.8 copy.43
  30.0 4.5 %reduce_max.19 = f32[192,64]{1,0:T(8,128)S(1)} reduce(f32[192,64,128]{2,1,0:T(8,128)} %bitcast.53, f32[]{:T(128)} %constant.5.clone.1), dimensions={2}, to_apply=%region_6.7 | reduce | flops 1560576 | bytes 6340612 | tf_op jit(solution)/shard_map/reduce_max | solution.py:64
  34.5 0.0 copy-start.2
  34.5 0.0 copy-start.3
  34.5 1.8 div.29
  36.3 0.1 copy-done.2
  36.4 1.0 copy-done.3
  37.3 6.5 %fusion.7 = bf16[192,8192]{1,0:T(8,128)(2,1)} fusion(bf16[192,8192]{1,0:T(8,128)(2,1)S(1)} %copy-done.2, f32[24,8,64,128]{3,2,1,0:T(8,128)S(1)} %bitcast.54, bf16[1,192,8192]{2,1,0:T(8,128)(2,1)S(1)} %copy-done.3), kind=kLoop, calls=%fused_computation.12 | loop fusion | flops 12582912 | bytes 15728640 | tf_op jit(solution)/shard_map/convert_element_type | solution.py:70
  43.8 0.0 reduce-scatter.8.cloned.1.call-update
  43.9 0.0 reduce-scatter.4.cloned.1.call-start
  43.9 65.3 %all-to-all-done = bf16[384,8,1024]{0,2,1:T(8,128)(2,1)} async-done(((bf16[384,8,1024]{0,2,1:T(8,128)(2,1)}), bf16[384,8,1024]{0,2,1:T(8,128)(2,1)}, u32[]{:S(2)}, u32[]{:S(2)}) %all-to-all-start) | async-done | bytes 6291488 | tf_op jit(solution)/shard_map/all_to_all | solution.py:54
  109.2 8.7 %copy.30 = bf16[8,384,1024]{2,1,0:T(8,128)(2,1)} copy(bf16[8,384,1024]{1,2,0:T(8,128)(2,1)} %bitcast.1) | data formatting | bytes 12582912 | tf_op jit(solution)/shard_map/all_to_all | solution.py:54
  117.9 0.0 copy-done
  117.9 12.5 %fusion.11 = f32[3072,1024]{1,0:T(8,128)} fusion(bf16[3072,1024]{1,0:T(8,128)(2,1)} %bitcast.56, bf16[1,1024,1024]{2,1,0:T(8,128)(2,1)S(1)} %copy-done), kind=kOutput, calls=%fused_computation.18 | convolution fusion | flops 6442450944 | bytes 20971520 | tf_op jit(solution)/shard_map/dot_general | solution.py:56
  130.4 0.0 copy-start.4
  130.4 0.0 reduce-scatter.4.cloned.1.call-update
  130.4 0.0 copy-start.6
  130.4 0.2 all-gather.2.cloned.1.call-start
  130.6 1.4 reduce-scatter.8.cloned.1.call-done
  132.1 0.0 copy-done.4
  132.1 0.0 copy-done.5
  132.1 2.0 fusion.18
  134.1 0.0 all-gather.2.cloned.1.call-update
  134.1 0.0 reduce-scatter.6.cloned.1.call-start
  134.2 114.8 %reduce-scatter.4.cloned.1.call-done = f32[768,1024]{1,0:T(8,128)} async-done(((f32[3072,1024]{1,0:T(8,128)}), f32[768,1024]{1,0:T(8,128)}) %reduce-scatter.4.cloned.1.call-update) | async-done | bytes 3145744 | tf_op jit(solution)/shard_map/reduce_scatter | solution.py:17
  249.0 0.0 reduce-scatter.6.cloned.1.call-update
  249.0 4.4 %copy.42 = bf16[48,8,32,128]{3,2,1,0:T(8,128)(2,1)} copy(bf16[48,8,32,128]{3,1,2,0:T(8,128)(2,1)} %bitcast.57) | data formatting | bytes 6291456
  253.4 0.0 copy-done.6
  253.4 0.2 reduce-window.4
  253.6 0.1 convert_reduce_fusion
  253.7 0.1 fusion.13
  253.8 52.4 %all-gather.2.cloned.1.call-done = bf16[192,8192]{1,0:T(8,128)(2,1)} async-done(((bf16[192,512]{1,0:T(8,128)(2,1)}), bf16[192,8192]{1,0:T(8,128)(2,1)}) %all-gather.2.cloned.1.call-update) | async-done | bytes 3145744 | tf_op jit(solution)/shard_map/all_gather | solution.py:75
  306.2 46.3 %reduce-scatter.6.cloned.1.call-done = f32[384,1024]{1,0:T(8,128)} async-done(((f32[768,1024]{1,0:T(8,128)}), f32[384,1024]{1,0:T(8,128)}) %reduce-scatter.6.cloned.1.call-update) | async-done | bytes 1572880 | tf_op jit(solution)/shard_map/reduce_scatter | solution.py:17
  352.5 1.5 convert_element_type.66
  354.0 0.1 fusion.19
  354.1 0.2 copy.39
  354.3 0.1 reshape.95
  354.4 11.2 %fusion.8 = f32[4,384,384,8]{2,1,3,0:T(8,128)} fusion(bf16[384,4,8,128]{3,2,1,0:T(8,128)(2,1)} %bitcast.55, bf16[384,4,128,1]{2,1,0,3:T(4,128)(2,1)S(1)} %bitcast.59), kind=kOutput, calls=%fused_computation.15 | convolution fusion | flops 1207959552 | bytes 22413312 | tf_op jit(solution)/shard_map/tgjd,sgd->gjts/dot_general | solution.py:36
  365.7 22.6 %fusion.20 = (f32[4,8,384]{2,1,0:T(8,128)S(1)}, f32[4,8,384,384]{2,3,1,0:T(8,128)}) fusion(f32[4,384,384,8]{2,1,3,0:T(8,128)} %fusion.8, pred[384,384]{0,1:T(8,128)(4,1)S(1)} %fusion.13), kind=kOutput, calls=%fused_computation.35 | output fusion | flops 28311936 | bytes 37945344 | tf_op jit(solution)/shard_map/sub | solution.py:42
  388.3 9.8 %fusion.10 = bf16[4,128,8,384]{3,1,2,0:T(8,128)(2,1)} fusion(bf16[384,4,128,1]{0,2,3,1:T(8,128)(2,1)S(1)} %bitcast.60, f32[4,8,384,384]{2,3,1,0:T(8,128)} %get-tuple-element.26, f32[4,8,384]{2,1,0:T(8,128)S(1)} %get-tuple-element.25), kind=kOutput, calls=%fused_computation.17 | convolution fusion | flops 1218969600 | bytes 22462464 | tf_op jit(solution)/shard_map/gjts,sgd->tgjd/dot_general | solution.py:44
  398.1 4.8 %copy.35 = bf16[1,384,4096]{2,1,0:T(8,128)(2,1)} copy(bf16[1,384,4096]{1,2,0:T(8,128)(2,1)} %bitcast.58) | data formatting | bytes 6291456
  402.9 3.9 copy.51
  406.8 0.0 copy-done.1
  (4 shorter events, 0.0 us)
Async XLA Ops:
  7.2 110.7 %copy-start = (bf16[1,1024,1024]{2,1,0:T(8,128)(2,1)S(1)}, bf16[1,1024,1024]{2,1,0:T(8,128)(2,1)}, u32[]{:S(2)}) copy-start(bf16[1,1024,1024]{2,1,0:T(8,128)(2,1)} %param.10) | copy-start | bytes 6291460
  16.0 93.2 %all-to-all-start = ((bf16[384,8,1024]{0,2,1:T(8,128)(2,1)}), bf16[384,8,1024]{0,2,1:T(8,128)(2,1)}, u32[]{:S(2)}, u32[]{:S(2)}) async-start(bf16[384,8,1024]{0,2,1:T(8,128)(2,1)} %bitcast.52), calls=%async_computation | async-start | bytes 12582912 | tf_op jit(solution)/shard_map/all_to_all | solution.py:54
  22.2 109.9 %reduce-scatter.8.cloned.1.call-start = ((), (), s32[]{:S(2)}) async-start(), calls=%async_computation.6 | async-start | bytes 3342336 | tf_op jit(solution)/shard_map/reduce_scatter | solution.py:69
  34.5 1.9 copy-start.2
  34.5 2.8 copy-start.3
  43.9 205.1 %reduce-scatter.4.cloned.1.call-start = ((), (), s32[]{:S(2)}) async-start(), calls=%async_computation.4 | async-start | bytes 15728640 | tf_op jit(solution)/shard_map/reduce_scatter | solution.py:17
  130.4 1.7 copy-start.4
  130.4 1.7 copy-start.5
  130.4 123.0 %copy-start.6 = (s32[1,1,6]{2,1,0:T(1,128)S(1)}, s32[1,1,6]{2,1,0:T(1,128)}, u32[]{:S(2)}) copy-start(s32[1,1,6]{2,1,0:T(1,128)} %param.11) | copy-start | bytes 76
  130.4 175.8 %all-gather.2.cloned.1.call-start = ((), (), s32[]{:S(2)}) async-start(), calls=%async_computation.7 | async-start | bytes 3342336 | tf_op jit(solution)/shard_map/all_gather | solution.py:75
  134.1 218.4 %reduce-scatter.6.cloned.1.call-start = ((), (), s32[]{:S(2)}) async-start(), calls=%async_computation.5 | async-start | bytes 4718592 | tf_op jit(solution)/shard_map/reduce_scatter | solution.py:17
  398.1 8.6 %copy-start.1 = (bf16[1,1024,1024]{2,1,0:T(8,128)(2,1)S(1)}, bf16[1,1024,1024]{2,1,0:T(8,128)(2,1)}, u32[]{:S(2)}) copy-start(bf16[1,1024,1024]{2,1,0:T(8,128)(2,1)} %param.10) | copy-start | bytes 6291460
Sparse Core Ops, SparseCore 0:
  44.0 88.0 reduce-scatter.7
  134.5 114.3 reduce-scatter.3
  251.8 54.3 all-gather.1
  308.4 44.0 reduce-scatter.5
where the time goes:
time: 414 us; the launch traced here: 413 us
  waiting for transfers between devices  280 us (68%)
  other arithmetic  41.5 us (10%)
  local copies, waits for them, and re-layouts  37.5 us (9%)
  matrix products  33.6 us (8%)
  between operations  13.9 us (3%)
  starting transfers between devices  6.55 us (2%)
    reduce_scatter x2, waiting for transfers between devices, summed_rows(): total = lax.psum_scatter(total, axis, scatter_dimension=0, tiled=True)  161 us
    all_to_all x1, waiting for transfers between devices, shards(): lax.all_to_all(own_tokens, FSDP, split_axis=1, concat_axis=0, tiled=True)  65.3 us
    all_gather x1, waiting for transfers between devices, shards(): lax.all_gather(new_master.astype(jnp.bfloat16), 'replica', axis=1, tiled=...  52.4 us
    unnamed x19, local copies, waits for them, and re-layouts  26.7 us
    sub x1, other arithmetic, attend(): expo = jnp.exp(scores - highest)  22.6 us
    dot_general x1, matrix products, shards(): jnp.dot(columns, weight_shard, preferred_element_type=jnp.float32)  12.5 us
    dot_general x1, matrix products, attend(): jnp.einsum('tgjd,sgd->gjts', grouped, key_heads, preferred_element_type=j...  11.2 us
    dot_general x1, matrix products, attend(): jnp.einsum('gjts,sgd->tgjd', attn_weights, value_heads, preferred_element...  9.84 us
  transfers between devices with their start and end apart: 5, of which 5 were waited for; matrix products, arithmetic and copies ran while one was open for 12% of the time, Pallas kernels for 0%

commit v1 on v0

--- a/solution.py
+++ b/solution.py
@@ -72,7 +72,12 @@
     averaged = summed * (1.0 / replicas)
     new_momentum = MOMENTUM_COEF * momentum + averaged
     new_master = master - OUTER_RATE * (averaged + MOMENTUM_COEF * new_momentum)
-    fresh_params = lax.all_gather(new_master.astype(jnp.bfloat16), "replica", axis=1, tiled=True)
+    fresh_params = jnp.concatenate(
+        lax.all_to_all(
+            jnp.stack([new_master.astype(jnp.bfloat16)] * lax.axis_size("replica")), "replica", 0, 0
+        ),
+        axis=1,
+    )
     return (attended, new_master, new_momentum, fresh_params)
 
 

time: 414 us -> 449 us (1.085)
  blocking collectives: 0 us -> 77.6 us
  waiting for transfers between devices: 280 us -> 235 us
    all_to_all x0 -> x1, blocking collectives: none -> 77.6 us  [shards(): lax.all_to_all(own_tokens, FSDP, split_axis=1, concat_axis=0, tiled=True)]
    reduce_scatter x1, waiting for transfers between devices: 1.43 us -> 78.4 us  [shards(): lax.psum_scatter(decoded.astype(jnp.bfloat16), 'replica', scatter_dimensi...]
    all_gather x1 -> x0, waiting for transfers between devices: 52.4 us -> none  [shards(): lax.all_gather(new_master.astype(jnp.bfloat16), 'replica', axis=1, tiled=...]
    reduce_scatter x2, waiting for transfers between devices: 161 us -> 115 us  [summed_rows(): total = lax.psum_scatter(total, axis, scatter_dimension=0, tiled=True)]
    all_to_all x1, waiting for transfers between devices: 65.3 us -> 40.6 us  [shards(): lax.all_to_all(jnp.stack([new_master.astype(jnp.bfloat16)] * lax.axis_siz...]
    unnamed x19 -> x18, local copies, waits for them, and re-layouts: 26.7 us -> 23.6 us
  transfers between devices with their start and end apart: 5 -> 4, of which waited for: 5 -> 4; matrix products, arithmetic and copies ran while one was open for 12% -> 8% of each run, Pallas kernels for 0% -> 0%
where the time goes in v1:
time: 449 us; the launch traced here: 448 us
  waiting for transfers between devices  235 us (52%)
  blocking collectives  77.6 us (17%)
  other arithmetic  41.9 us (9%)
  local copies, waits for them, and re-layouts  40.3 us (9%)
  matrix products  33.6 us (7%)
  between operations  13.8 us (3%)
  starting transfers between devices  6.48 us (1%)
    reduce_scatter x2, waiting for transfers between devices, summed_rows(): total = lax.psum_scatter(total, axis, scatter_dimension=0, tiled=True)  115 us
    reduce_scatter x1, waiting for transfers between devices, shards(): lax.psum_scatter(decoded.astype(jnp.bfloat16), 'replica', scatter_dimensi...  78.4 us
    all_to_all x1, blocking collectives, shards(): lax.all_to_all(own_tokens, FSDP, split_axis=1, concat_axis=0, tiled=True)  77.6 us
    all_to_all x1, waiting for transfers between devices, shards(): lax.all_to_all(jnp.stack([new_master.astype(jnp.bfloat16)] * lax.axis_siz...  40.6 us
    unnamed x18, local copies, waits for them, and re-layouts  23.6 us
    sub x1, other arithmetic, attend(): expo = jnp.exp(scores - highest)  23.1 us
    dot_general x1, matrix products, shards(): jnp.dot(columns, weight_shard, preferred_element_type=jnp.float32)  12.4 us
    dot_general x1, matrix products, attend(): jnp.einsum('tgjd,sgd->gjts', grouped, key_heads, preferred_element_type=j...  11.2 us
  transfers between devices with their start and end apart: 4, of which 4 were waited for; matrix products, arithmetic and copies ran while one was open for 8% of the time, Pallas kernels for 0%

profile of v1, /device:TPU:1, one launch (start us, length us, event | category | flops | bytes accessed | tf_op | source)
XLA Modules:
  0.0 448.3 jit_solution(15789187238926468514)
XLA Ops:
  7.2 0.0 copy-start
  7.2 0.0 reduce-scatter.4.cloned.1.call-start
  7.2 8.8 %copy.44 = bf16[1,384,8192]{1,2,0:T(8,128)(2,1)} copy(bf16[1,384,8192]{2,1,0:T(8,128)(2,1)} %param.8) | data formatting | bytes 12582912 | tf_op args[0]
  16.0 77.6 %all_to_all.24 = bf16[384,8,1024]{0,2,1:T(8,128)(2,1)} all-to-all(bf16[384,8,1024]{0,2,1:T(8,128)(2,1)} %bitcast.57), channel_id=1, replica_groups=mesh['replica'=16,'fsdp_0'=4,'fsdp_1'=2] {'fsdp_0','fsdp_1'}, dimensions={1} | all-to-all | bytes 12582912 | tf_op jit(solution)/shard_map/all_to_all | solution.py:54
  93.6 8.7 %copy.45 = bf16[8,384,1024]{2,1,0:T(8,128)(2,1)} copy(bf16[8,384,1024]{1,2,0:T(8,128)(2,1)} %bitcast.56) | data formatting | bytes 12582912 | tf_op jit(solution)/shard_map/all_to_all | solution.py:54
  102.3 0.0 copy-done
  102.3 12.4 %fusion.11 = f32[3072,1024]{1,0:T(8,128)} fusion(bf16[3072,1024]{1,0:T(8,128)(2,1)} %bitcast.60, bf16[1,1024,1024]{2,1,0:T(8,128)(2,1)S(1)} %copy-done), kind=kOutput, calls=%fused_computation.18 | convolution fusion | flops 6442450944 | bytes 20971520 | tf_op jit(solution)/shard_map/dot_general | solution.py:56
  114.7 0.0 reduce-scatter.4.cloned.1.call-update
  114.7 0.0 reduce-scatter.8.cloned.1.call-start
  114.8 4.0 abs_bitcast_fusion
  118.7 3.8 copy.60
  122.5 4.5 reduce_max.19
  127.0 0.0 copy-start.2
  127.0 0.0 copy-start.3
  127.1 1.8 div.29
  128.8 0.1 copy-done.2
  129.0 0.9 copy-done.3
  129.9 6.5 %fusion.7 = bf16[192,8192]{1,0:T(8,128)(2,1)} fusion(bf16[192,8192]{1,0:T(8,128)(2,1)S(1)} %copy-done.2, f32[24,8,64,128]{3,2,1,0:T(8,128)S(1)} %bitcast.58, bf16[1,192,8192]{2,1,0:T(8,128)(2,1)S(1)} %copy-done.3), kind=kLoop, calls=%fused_computation.12 | loop fusion | flops 12582912 | bytes 15728640 | tf_op jit(solution)/shard_map/convert_element_type | solution.py:70
  136.4 0.0 copy-start.4
  136.4 0.0 copy-start.5
  136.4 0.0 reduce-scatter.8.cloned.1.call-update
  136.5 0.2 reduce-scatter.6.cloned.1.call-start
  136.7 94.7 %reduce-scatter.4.cloned.1.call-done = f32[768,1024]{1,0:T(8,128)} async-done(((f32[3072,1024]{1,0:T(8,128)}), f32[768,1024]{1,0:T(8,128)}) %reduce-scatter.4.cloned.1.call-update) | async-done | bytes 3145744 | tf_op jit(solution)/shard_map/reduce_scatter | solution.py:17
  231.4 0.0 reduce-scatter.6.cloned.1.call-update
  231.4 78.4 %reduce-scatter.8.cloned.1.call-done = bf16[192,512]{1,0:T(8,128)(2,1)} async-done(((bf16[192,8192]{1,0:T(8,128)(2,1)}), bf16[192,512]{1,0:T(8,128)(2,1)}) %reduce-scatter.8.cloned.1.call-update) | async-done | bytes 196624 | tf_op jit(solution)/shard_map/reduce_scatter | solution.py:69
  309.8 0.0 copy-done.4
  309.8 0.0 copy-done.5
  309.8 1.9 fusion.18
  311.8 2.0 stack.2
  313.7 0.0 copy-start.6
  313.7 6.2 %all-to-all-start.1 = ((bf16[16,192,512]{2,1,0:T(8,128)(2,1)}), bf16[16,192,512]{2,1,0:T(8,128)(2,1)}, u32[]{:S(2)}, u32[]{:S(2)}) async-start(bf16[16,192,512]{2,1,0:T(8,128)(2,1)} %stack.2), calls=%async_computation.4 | async-start | bytes 6291456 | tf_op jit(solution)/shard_map/all_to_all | solution.py:76
  319.9 5.2 %copy.59 = bf16[48,8,32,128]{3,2,1,0:T(8,128)(2,1)} copy(bf16[48,8,32,128]{3,1,2,0:T(8,128)(2,1)} %bitcast.61) | data formatting | bytes 6291456
  325.2 0.0 copy-done.6
  325.2 0.2 reduce-window.4
  325.4 0.1 convert_reduce_fusion
  325.4 0.1 fusion.13
  325.6 40.6 %all-to-all-done.1 = bf16[16,192,512]{2,1,0:T(8,128)(2,1)} async-done(((bf16[16,192,512]{2,1,0:T(8,128)(2,1)}), bf16[16,192,512]{2,1,0:T(8,128)(2,1)}, u32[]{:S(2)}, u32[]{:S(2)}) %all-to-all-start.1) | async-done | bytes 3145760 | tf_op jit(solution)/shard_map/all_to_all | solution.py:76
  366.2 3.9 copy.58
  370.1 20.8 %reduce-scatter.6.cloned.1.call-done = f32[384,1024]{1,0:T(8,128)} async-done(((f32[768,1024]{1,0:T(8,128)}), f32[384,1024]{1,0:T(8,128)}) %reduce-scatter.6.cloned.1.call-update) | async-done | bytes 1572880 | tf_op jit(solution)/shard_map/reduce_scatter | solution.py:17
  391.0 1.5 convert_element_type.66
  392.5 0.1 fusion.19
  392.5 0.2 copy.55
  392.8 0.1 reshape.103
  392.9 11.2 %fusion.8 = f32[4,384,384,8]{2,1,3,0:T(8,128)} fusion(bf16[384,4,8,128]{3,2,1,0:T(8,128)(2,1)} %bitcast.59, bf16[384,4,128,1]{2,1,0,3:T(4,128)(2,1)S(1)} %bitcast.64), kind=kOutput, calls=%fused_computation.15 | convolution fusion | flops 1207959552 | bytes 22413312 | tf_op jit(solution)/shard_map/tgjd,sgd->gjts/dot_general | solution.py:36
  404.1 23.1 %fusion.20 = (f32[4,8,384]{2,1,0:T(8,128)S(1)}, f32[4,8,384,384]{2,3,1,0:T(8,128)}) fusion(f32[4,384,384,8]{2,1,3,0:T(8,128)} %fusion.8, pred[384,384]{0,1:T(8,128)(4,1)S(1)} %fusion.13), kind=kOutput, calls=%fused_computation.35 | output fusion | flops 28311936 | bytes 37945344 | tf_op jit(solution)/shard_map/sub | solution.py:42
  427.2 10.0 %fusion.10 = bf16[4,128,8,384]{3,1,2,0:T(8,128)(2,1)} fusion(bf16[384,4,128,1]{0,2,3,1:T(8,128)(2,1)S(1)} %bitcast.65, f32[4,8,384,384]{2,3,1,0:T(8,128)} %get-tuple-element.34, f32[4,8,384]{2,1,0:T(8,128)S(1)} %get-tuple-element.33), kind=kOutput, calls=%fused_computation.17 | convolution fusion | flops 1218969600 | bytes 22462464 | tf_op jit(solution)/shard_map/gjts,sgd->tgjd/dot_general | solution.py:44
  437.2 4.6 %copy.51 = bf16[1,384,4096]{2,1,0:T(8,128)(2,1)} copy(bf16[1,384,4096]{1,2,0:T(8,128)(2,1)} %bitcast.63) | data formatting | bytes 6291456
  441.8 0.0 copy-done.1
  (3 shorter events, 0.0 us)
Async XLA Ops:
  7.2 95.2 %copy-start = (bf16[1,1024,1024]{2,1,0:T(8,128)(2,1)S(1)}, bf16[1,1024,1024]{2,1,0:T(8,128)(2,1)}, u32[]{:S(2)}) copy-start(bf16[1,1024,1024]{2,1,0:T(8,128)(2,1)} %param.10) | copy-start | bytes 6291460
  7.2 224.2 %reduce-scatter.4.cloned.1.call-start = ((), (), s32[]{:S(2)}) async-start(), calls=%async_computation.5 | async-start | bytes 15728640 | tf_op jit(solution)/shard_map/reduce_scatter | solution.py:17
  114.7 195.1 %reduce-scatter.8.cloned.1.call-start = ((), (), s32[]{:S(2)}) async-start(), calls=%async_computation.7 | async-start | bytes 3342336 | tf_op jit(solution)/shard_map/reduce_scatter | solution.py:69
  127.0 2.0 copy-start.2
  127.0 2.9 copy-start.3
  136.4 173.4 %copy-start.4 = (f32[192,512]{1,0:T(8,128)S(1)}, f32[192,512]{1,0:T(8,128)}, u32[]{:S(2)}) copy-start(f32[192,512]{1,0:T(8,128)} %param.14) | copy-start | bytes 1179652
  136.4 173.4 %copy-start.5 = (f32[192,512]{1,0:T(8,128)S(1)}, f32[192,512]{1,0:T(8,128)}, u32[]{:S(2)}) copy-start(f32[192,512]{1,0:T(8,128)} %param.15) | copy-start | bytes 1179652
  136.5 254.5 %reduce-scatter.6.cloned.1.call-start = ((), (), s32[]{:S(2)}) async-start(), calls=%async_computation.6 | async-start | bytes 4718592 | tf_op jit(solution)/shard_map/reduce_scatter | solution.py:17
  313.7 11.4 %copy-start.6 = (s32[1,1,6]{2,1,0:T(1,128)S(1)}, s32[1,1,6]{2,1,0:T(1,128)}, u32[]{:S(2)}) copy-start(s32[1,1,6]{2,1,0:T(1,128)} %param.11) | copy-start | bytes 76
  313.7 52.5 %all-to-all-start.1 = ((bf16[16,192,512]{2,1,0:T(8,128)(2,1)}), bf16[16,192,512]{2,1,0:T(8,128)(2,1)}, u32[]{:S(2)}, u32[]{:S(2)}) async-start(bf16[16,192,512]{2,1,0:T(8,128)(2,1)} %stack.2), calls=%async_computation.4 | async-start | bytes 6291456 | tf_op jit(solution)/shard_map/all_to_all | solution.py:76
  427.1 14.7 %copy-start.1 = (bf16[1,1024,1024]{2,1,0:T(8,128)(2,1)S(1)}, bf16[1,1024,1024]{2,1,0:T(8,128)(2,1)}, u32[]{:S(2)}) copy-start(bf16[1,1024,1024]{2,1,0:T(8,128)(2,1)} %param.10) | copy-start | bytes 6291460
Sparse Core Ops, SparseCore 0:
  114.8 116.4 reduce-scatter.3
  236.0 73.8 reduce-scatter.7
  312.2 78.7 reduce-scatter.5
